TPU v7x, 32 devices: a whole 2x2x4 slice. The times are simulated.
32 devices in a mesh: groups: 2 (over y), brow: 8 (over z, x), bcol: 2 (over core).
Axes of the slice: x: 2, y: 2, z: 4, core: 2. Of those that a mesh axis runs over, the one named last changes fastest.
Arguments:
- near_pairs: int32 [2048, 2], P(('groups', 'brow', 'bcol')), parts along dimension 0, may hold values from 0 to 255, as said below
- rule_orders: int32 [2048], P(('groups', 'brow', 'bcol')), parts along dimension 0, may hold values from 1 to 3, as said below
- geometry: float32 [6, 131072], P(None, ('groups', 'brow')), parts along dimension 1, may hold values from -1 to 1
- resist: float32 [131072], P(('groups', 'brow')), parts along dimension 0, may hold values from 0.5 to 2
- laplace: float32 [32], replicated, may hold values from 0.002 to 0.02
- right_sides: float32 [32, 131072], P(None, ('groups', 'brow')), parts along dimension 1, may hold values from -40 to 40
Outputs:
- solution: float32 [32, 131072], P(None, ('groups', 'brow')), parts along dimension 1
There are 2 independent parts, one for each index of `groups`. A program takes and returns all parts, laid end to end along the dimension named above; an argument that names none is the same for every part. Nothing has to cross between parts.
Inputs may be any that keep to these rules, and one draw needn't show every extreme that they name: `near_pairs`: the row block i of each pair is owned by brow index i // 32, the brow index of the device that holds the pair; among the 64 pairs of one device at most 16 have column blocks of one owner (column block // 32), and on every device some owner has exactly 16. `rule_orders`: orders may differ from pair to pair and from device to device.
All inputs are finite; a program needn't handle non-finite values.
Results may differ from a plain program's by a relative error of at most 0.0003.
Values sent between devices are 32-bit elements; how exact they have to be, the bound alone decides.
A program may use at most 192 MiB of HBM per device.

v0:
```python
from functools import partial
import math

import jax
import jax.numpy as jnp
from jax import lax
from jax.sharding import PartitionSpec as P

BS = 256


RADIUS_SQUARED = 0.0025
GAUSS_TWO = 0.5 / math.sqrt(3.0)
GAUSS_THREE = math.sqrt(0.15)
NODE_TABLE = ((0.0, 0.0, 0.0), (-GAUSS_TWO, GAUSS_TWO, 0.0), (-GAUSS_THREE, 0.0, GAUSS_THREE))
WEIGHT_TABLE = ((1.0, 0.0, 0.0), (0.5, 0.5, 0.0), (5.0 / 18.0, 8.0 / 18.0, 5.0 / 18.0))
EPSILON = 1e-12
PRECISE = lax.Precision.HIGHEST


def rule_terms(rule_orders):
    chosen = (rule_orders[:, None] == jnp.arange(1, 4, dtype=jnp.int32)[None, :]).astype(
        jnp.float32
    )
    abscissa = jnp.dot(chosen, jnp.array(NODE_TABLE, jnp.float32), precision=PRECISE)
    weights = jnp.dot(chosen, jnp.array(WEIGHT_TABLE, jnp.float32), precision=PRECISE)
    return (abscissa, weights)


def block_kernel(left_geometry, right_geometry, rule_orders, terms_used):
    abscissa, weights = rule_terms(rule_orders)
    shape_out = (left_geometry.shape[0], left_geometry.shape[2], right_geometry.shape[2])
    summed = jnp.zeros(shape_out, jnp.float32)
    for first_node in range(terms_used):
        for second_node in range(terms_used):
            squared = jnp.full(shape_out, RADIUS_SQUARED, jnp.float32)
            for component in range(3):
                point_left = (
                    left_geometry[:, component, :]
                    + abscissa[:, first_node : first_node + 1] * left_geometry[:, component + 3, :]
                )
                point_right = (
                    right_geometry[:, component, :]
                    + abscissa[:, second_node : second_node + 1]
                    * right_geometry[:, component + 3, :]
                )
                offset = point_left[:, :, None] - point_right[:, None, :]
                squared = squared + offset * offset
            factor = (weights[:, first_node] * weights[:, second_node])[:, None, None]
            summed = summed + factor * lax.rsqrt(squared)
    tangents = jnp.einsum(
        "gda,gdb->gab", left_geometry[:, 3:6, :], right_geometry[:, 3:6, :], precision=PRECISE
    )
    return tangents * summed


def build_blocks(left_geometry, right_geometry, rule_orders):
    total_pairs = rule_orders.shape[0]
    group_size = math.gcd(total_pairs, 8)
    batches = total_pairs // group_size
    block_width = left_geometry.shape[2]
    branches = [partial(block_kernel, terms_used=rule_level) for rule_level in (1, 2, 3)]

    def one_group(packed):
        left_part, right_part, order_part = packed
        highest = jnp.clip(jnp.max(order_part), 1, 3) - 1
        return lax.switch(highest, branches, left_part, right_part, order_part)

    packed = (
        left_geometry.reshape(batches, group_size, 6, block_width),
        right_geometry.reshape(batches, group_size, 6, block_width),
        rule_orders.reshape(batches, group_size),
    )
    assembled = lax.map(one_group, packed)
    return assembled.reshape(total_pairs, block_width, block_width)


def body(near_pairs, rule_orders, geometry, resist, laplace, right_sides):
    owners = lax.axis_size("brow")
    here = lax.axis_index("brow")
    block_width = BS
    blocks_here = geometry.shape[1] // block_width
    rhs_count = right_sides.shape[0]
    pair_count = near_pairs.shape[0]
    capacity = max(2, 2 * pair_count // owners)
    slot_count = owners * capacity
    own_geometry = geometry.reshape(6, blocks_here, block_width).transpose(1, 0, 2)
    row_local = near_pairs[:, 0] - here * blocks_here
    column_owner = near_pairs[:, 1] // blocks_here
    column_local = near_pairs[:, 1] % blocks_here
    owner_hits = (column_owner[:, None] == jnp.arange(owners, dtype=jnp.int32)[None, :]).astype(
        jnp.int32
    )
    earlier = jnp.cumsum(owner_hits, axis=0) - owner_hits
    slot_of = column_owner * capacity + jnp.sum(earlier * owner_hits, axis=1)
    distinct = (near_pairs[:, 0] != near_pairs[:, 1]).astype(jnp.int32)
    row_hot = (jnp.arange(blocks_here, dtype=jnp.int32)[:, None] == row_local[None, :]).astype(
        jnp.float32
    )
    row_geometry = own_geometry[row_local]
    request_table = jnp.full((slot_count,), -1, jnp.int32).at[slot_of].set(column_local)
    incoming = lax.all_to_all(
        request_table.reshape(owners, capacity), "brow", split_axis=0, concat_axis=0, tiled=True
    ).reshape(slot_count)
    served = jnp.maximum(incoming, 0)
    live = (incoming >= 0).astype(jnp.float32)
    serve_hot = (jnp.arange(blocks_here, dtype=jnp.int32)[:, None] == incoming[None, :]).astype(
        jnp.float32
    )
    give_geometry = (own_geometry[served] * live[:, None, None]).reshape(
        owners, capacity, 6, block_width
    )
    column_geometry = lax.all_to_all(
        give_geometry, "brow", split_axis=0, concat_axis=0, tiled=True
    ).reshape(slot_count, 6, block_width)[slot_of]
    blocks = build_blocks(row_geometry, column_geometry, rule_orders)
    distinct_float = distinct.astype(jnp.float32)
    resist_blocks = resist.reshape(blocks_here, 1, block_width)
    laplace_rows = laplace.reshape(1, rhs_count, 1)

    def apply_operator(vector):
        give = (vector[served] * live[:, None, None]).reshape(
            owners, capacity, rhs_count, block_width
        )
        row_vectors = vector[row_local]
        fetched = lax.all_to_all(give, "brow", split_axis=0, concat_axis=0, tiled=True)
        column_vectors = fetched.reshape(slot_count, rhs_count, block_width)[slot_of]
        forward = jnp.einsum("pab,pfb->pfa", blocks, column_vectors, precision=PRECISE)
        transposed = (
            jnp.einsum("pab,pfa->pfb", blocks, row_vectors, precision=PRECISE)
            * distinct_float[:, None, None]
        )
        send_back = (
            jnp.zeros((slot_count, rhs_count, block_width), jnp.float32).at[slot_of].set(transposed)
        )
        backward = lax.all_to_all(
            send_back.reshape(owners, capacity, rhs_count, block_width),
            "brow",
            split_axis=0,
            concat_axis=0,
            tiled=True,
        ).reshape(slot_count, rhs_count, block_width)
        local_terms = jnp.einsum("kp,pfa->kfa", row_hot, forward, precision=PRECISE) + jnp.einsum(
            "ks,sfa->kfa", serve_hot, backward, precision=PRECISE
        )
        near_sum = lax.psum(local_terms, "bcol")
        return resist_blocks * vector + laplace_rows * near_sum

    def product(left, right):
        return jnp.sum(left * right, axis=(0, 2))

    start = right_sides.reshape(rhs_count, blocks_here, block_width).transpose(1, 0, 2)
    start_norm = jnp.sqrt(lax.psum(product(start, start), "brow") + EPSILON)
    first = start / start_norm[None, :, None]
    image = apply_operator(first)
    along_first = lax.psum(product(first, image), "brow")
    second_raw = image - along_first[None, :, None] * first
    rest_first = jnp.sqrt(lax.psum(product(second_raw, second_raw), "brow") + EPSILON)
    second = second_raw / rest_first[None, :, None]
    image_two = apply_operator(second)
    along_cross, along_second = lax.psum(
        (product(first, image_two), product(second, image_two)), "brow"
    )
    remainder = (
        image_two - along_cross[None, :, None] * first - along_second[None, :, None] * second
    )
    rest_second = jnp.sqrt(lax.psum(product(remainder, remainder), "brow") + EPSILON)
    radius_one = jnp.sqrt(along_first * along_first + rest_first * rest_first)
    cosine_one = along_first / radius_one
    sine_one = rest_first / radius_one
    upper_right = cosine_one * along_cross + sine_one * along_second
    lower_right = cosine_one * along_second - sine_one * along_cross
    radius_two = jnp.sqrt(lower_right * lower_right + rest_second * rest_second)
    amount_two = -(lower_right / radius_two) * start_norm * sine_one / radius_two
    amount_one = (start_norm * cosine_one - upper_right * amount_two) / radius_one
    combined = amount_one[None, :, None] * first + amount_two[None, :, None] * second
    return combined.transpose(1, 0, 2).reshape(rhs_count, blocks_here * block_width)


def solution(mesh):
    return jax.shard_map(
        body,
        mesh=mesh,
        in_specs=(
            P(("groups", "brow", "bcol"), None),
            P(("groups", "brow", "bcol")),
            P(None, ("groups", "brow")),
            P(("groups", "brow")),
            P(),
            P(None, ("groups", "brow")),
        ),
        out_specs=P(None, ("groups", "brow")),
        check_vma=False,
    )
```

profile of v0, /device:TPU:0, one launch (start us, length us, event | category | flops | bytes accessed | tf_op | source)
XLA Modules:
  0.0 652.3 jit_solution(14852295463436428467)
XLA Ops:
  9.8 13.5 %all_to_all.34 = s32[8,1,16]{2,1,0:T(1,128)S(1)} all-to-all(s32[8,1,16]{2,1,0:T(1,128)S(1)} %bitcast.311), channel_id=1, replica_groups=mesh['groups'=2,'brow'=8,'bcol'=2] {'brow'}, dimensions={0} | all-to-all | bytes 1024 | tf_op jit(solution)/shard_map/all_to_all | solution.py:102
  25.3 3.5 all-to-all-start.2
  30.8 24.7 %psum.56 = f32[32]{0:T(128)S(1)} all-reduce(f32[32]{0:T(128)S(1)} %fusion.53), channel_id=1, replica_groups=mesh['groups'=2,'brow'=8,'bcol'=2] {'brow'}, use_global_device_ids=true, to_apply=%region_1.2 | all-reduce | flops 32 | bytes 256 | tf_op jit(solution)/shard_map/psum | solution.py:153
  59.1 4.5 broadcast_multiply_fusion.1
  63.6 4.8 all-to-all-start.1
  72.4 76.6 %while.14 = (s32[]{:T(128)}, f32[8,8,256,256]{3,2,1,0:T(8,128)}, s32[8,8]{1,0:T(8,128)S(1)}, f32[8,8,6,256]{3,2,1,0:T(8,128)S(1)}, f32[8,8,6,256]{3,2,1,0:T(8,12...) while((s32[]{:T(128)}, f32[8,8,256,256]{3,2,1,0:T(8,128)}, ...), condition=%wide.region_10.11_spmd.clone.clone, body=%wide.region_5.10_spmd.sunk.clone.clone.sunk | while | flops 70854448 | bytes 7263025 | solution.py:74
  73.7 6.8 %conditional.5 = (f32[1,8,256,256]{3,2,1,0:T(8,128)S(1)}) conditional(s32[]{:T(128)} %clamp.22, (f32[8,6,256]{2,1,0:T(8,128)S(1)}, f32[8,6,256]{2,1,0:T(8,128)S(1)}, s32[8]{0:T(128)S(1)}, f32[3,3]{1,0:T(4,128)S(1)}, f32[3,3]{1,0:T(4,128)S(1)}) %tuple.114, (f32[8,6,256]{2,1,0:T(8,128)S(1)}, f32[8,6,256]{2,1,0:T(8,128)S(1)}, ...), branch_computations={%region_7.7_spmd, %region_8.8_spmd, %region_9.9_spmd} | conditional | flops 70854432 | bytes 2871316 | solution.py:67
  74.4 6.1 multiply_bitcast_fusion
  83.3 6.8 %conditional.5 = (f32[1,8,256,256]{3,2,1,0:T(8,128)S(1)}) conditional(s32[]{:T(128)} %clamp.22, (f32[8,6,256]{2,1,0:T(8,128)S(1)}, f32[8,6,256]{2,1,0:T(8,128)S(1)}, s32[8]{0:T(128)S(1)}, f32[3,3]{1,0:T(4,128)S(1)}, f32[3,3]{1,0:T(4,128)S(1)}) %tuple.114, (f32[8,6,256]{2,1,0:T(8,128)S(1)}, f32[8,6,256]{2,1,0:T(8,128)S(1)}, ...), branch_computations={%region_7.7_spmd, %region_8.8_spmd, %region_9.9_spmd} | conditional | flops 70854432 | bytes 2871316 | solution.py:67
  84.0 6.1 multiply_bitcast_fusion
  92.8 6.8 %conditional.5 = (f32[1,8,256,256]{3,2,1,0:T(8,128)S(1)}) conditional(s32[]{:T(128)} %clamp.22, (f32[8,6,256]{2,1,0:T(8,128)S(1)}, f32[8,6,256]{2,1,0:T(8,128)S(1)}, s32[8]{0:T(128)S(1)}, f32[3,3]{1,0:T(4,128)S(1)}, f32[3,3]{1,0:T(4,128)S(1)}) %tuple.114, (f32[8,6,256]{2,1,0:T(8,128)S(1)}, f32[8,6,256]{2,1,0:T(8,128)S(1)}, ...), branch_computations={%region_7.7_spmd, %region_8.8_spmd, %region_9.9_spmd} | conditional | flops 70854432 | bytes 2871316 | solution.py:67
  93.6 6.1 multiply_bitcast_fusion
  102.4 6.8 %conditional.5 = (f32[1,8,256,256]{3,2,1,0:T(8,128)S(1)}) conditional(s32[]{:T(128)} %clamp.22, (f32[8,6,256]{2,1,0:T(8,128)S(1)}, f32[8,6,256]{2,1,0:T(8,128)S(1)}, s32[8]{0:T(128)S(1)}, f32[3,3]{1,0:T(4,128)S(1)}, f32[3,3]{1,0:T(4,128)S(1)}) %tuple.114, (f32[8,6,256]{2,1,0:T(8,128)S(1)}, f32[8,6,256]{2,1,0:T(8,128)S(1)}, ...), branch_computations={%region_7.7_spmd, %region_8.8_spmd, %region_9.9_spmd} | conditional | flops 70854432 | bytes 2871316 | solution.py:67
  103.1 6.1 multiply_bitcast_fusion
  112.0 6.8 %conditional.5 = (f32[1,8,256,256]{3,2,1,0:T(8,128)S(1)}) conditional(s32[]{:T(128)} %clamp.22, (f32[8,6,256]{2,1,0:T(8,128)S(1)}, f32[8,6,256]{2,1,0:T(8,128)S(1)}, s32[8]{0:T(128)S(1)}, f32[3,3]{1,0:T(4,128)S(1)}, f32[3,3]{1,0:T(4,128)S(1)}) %tuple.114, (f32[8,6,256]{2,1,0:T(8,128)S(1)}, f32[8,6,256]{2,1,0:T(8,128)S(1)}, ...), branch_computations={%region_7.7_spmd, %region_8.8_spmd, %region_9.9_spmd} | conditional | flops 70854432 | bytes 2871316 | solution.py:67
  112.7 6.1 multiply_bitcast_fusion
  121.6 6.8 %conditional.5 = (f32[1,8,256,256]{3,2,1,0:T(8,128)S(1)}) conditional(s32[]{:T(128)} %clamp.22, (f32[8,6,256]{2,1,0:T(8,128)S(1)}, f32[8,6,256]{2,1,0:T(8,128)S(1)}, s32[8]{0:T(128)S(1)}, f32[3,3]{1,0:T(4,128)S(1)}, f32[3,3]{1,0:T(4,128)S(1)}) %tuple.114, (f32[8,6,256]{2,1,0:T(8,128)S(1)}, f32[8,6,256]{2,1,0:T(8,128)S(1)}, ...), branch_computations={%region_7.7_spmd, %region_8.8_spmd, %region_9.9_spmd} | conditional | flops 70854432 | bytes 2871316 | solution.py:67
  122.3 6.1 multiply_bitcast_fusion
  131.2 6.8 %conditional.5 = (f32[1,8,256,256]{3,2,1,0:T(8,128)S(1)}) conditional(s32[]{:T(128)} %clamp.22, (f32[8,6,256]{2,1,0:T(8,128)S(1)}, f32[8,6,256]{2,1,0:T(8,128)S(1)}, s32[8]{0:T(128)S(1)}, f32[3,3]{1,0:T(4,128)S(1)}, f32[3,3]{1,0:T(4,128)S(1)}) %tuple.114, (f32[8,6,256]{2,1,0:T(8,128)S(1)}, f32[8,6,256]{2,1,0:T(8,128)S(1)}, ...), branch_computations={%region_7.7_spmd, %region_8.8_spmd, %region_9.9_spmd} | conditional | flops 70854432 | bytes 2871316 | solution.py:67
  131.9 6.1 multiply_bitcast_fusion
  140.8 6.8 %conditional.5 = (f32[1,8,256,256]{3,2,1,0:T(8,128)S(1)}) conditional(s32[]{:T(128)} %clamp.22, (f32[8,6,256]{2,1,0:T(8,128)S(1)}, f32[8,6,256]{2,1,0:T(8,128)S(1)}, s32[8]{0:T(128)S(1)}, f32[3,3]{1,0:T(4,128)S(1)}, f32[3,3]{1,0:T(4,128)S(1)}) %tuple.114, (f32[8,6,256]{2,1,0:T(8,128)S(1)}, f32[8,6,256]{2,1,0:T(8,128)S(1)}, ...), branch_computations={%region_7.7_spmd, %region_8.8_spmd, %region_9.9_spmd} | conditional | flops 70854432 | bytes 2871316 | solution.py:67
  141.5 6.1 multiply_bitcast_fusion
  149.0 13.4 %convolution_multiply_fusion.2 = f32[64,32,256]{2,1,0:T(8,128)S(1)} fusion(f32[64,32,256]{2,1,0:T(8,128)} %gather_fusion.5, f32[64,256,256]{2,1,0:T(8,128)} %bitcast.290, f32[64]{0:T(128)S(1)} %fusion.67), kind=kOutput, calls=%fused_computation.155 | convolution fusion | flops 1611137024 | bytes 20971776 | tf_op jit(solution)/shard_map/pab,pfa->pfb/dot_general | solution.py:130
  164.9 8.6 %scatter_fusion = f32[128,32,256]{2,1,0:T(8,128)} fusion(f32[128,32,256]{2,1,0:T(8,128)} %broadcast.410.clone, s32[64]{0:T(128)S(1)} %fusion.69, f32[64,32,256]{2,1,0:T(8,128)S(1)} %convolution_multiply_fusion.2), kind=kCustom, calls=%fused_computation.10 | custom fusion | bytes 6291712 | tf_op jit(solution)/shard_map/scatter | solution.py:134
  173.6 6.6 %copy.104 = f32[8,16,32,256]{3,1,2,0:T(8,128)} copy(f32[8,16,32,256]{3,2,1,0:T(8,128)} %bitcast.295) | data formatting | bytes 8388608 | tf_op jit(solution)/shard_map/reshape | solution.py:137
  180.1 39.2 %all-to-all-start.3 = ((f32[8,16,32,256]{3,1,2,0:T(8,128)}), f32[8,16,32,256]{3,1,2,0:T(8,128)}, u32[]{:S(2)}, u32[]{:S(2)}) async-start(f32[8,16,32,256]{3,1,2,0:T(8,128)} %copy.104), calls=%async_computation.3 | async-start | bytes 8388608 | tf_op jit(solution)/shard_map/all_to_all | solution.py:136
  220.6 3.0 gather_fusion.1
  223.6 20.3 %fusion.74 = f32[64,32,256]{2,1,0:T(8,128)} fusion(f32[64,32,256]{2,1,0:T(8,128)S(1)} %gather_fusion.1, f32[64,256,256]{2,1,0:T(8,128)} %bitcast.291), kind=kOutput, calls=%fused_computation.216 | convolution fusion | flops 1610612736 | bytes 20971520 | tf_op jit(solution)/shard_map/pab,pfb->pfa/dot_general | solution.py:128
  243.9 65.8 %all-to-all-done.3 = f32[8,16,32,256]{3,1,2,0:T(8,128)} async-done(((f32[8,16,32,256]{3,1,2,0:T(8,128)}), f32[8,16,32,256]{3,1,2,0:T(8,128)}, u32[]{:S(2)}, u32[]{:S(2)}) %all-to-all-start.3) | async-done | bytes 4194336 | tf_op jit(solution)/shard_map/all_to_all | solution.py:136
  314.2 3.0 fusion.47
  317.3 17.9 %all-reduce.4.cloned.1.call-done = f32[32,32,256]{2,0,1:T(8,128)} async-done(((f32[32,32,256]{2,0,1:T(8,128)}), f32[32,32,256]{2,0,1:T(8,128)}) %all-reduce.4.cloned.1.call-update) | async-done | bytes 1048592 | tf_op jit(solution)/shard_map/psum | solution.py:146
  337.1 21.6 %psum.58 = f32[32]{0:T(128)S(1)} all-reduce(f32[32]{0:T(128)S(1)} %multiply_reduce_fusion.4), channel_id=1, replica_groups=mesh['groups'=2,'brow'=8,'bcol'=2] {'brow'}, use_global_device_ids=true, to_apply=%region_14.15 | all-reduce | flops 32 | bytes 256 | tf_op jit(solution)/shard_map/psum | solution.py:156
  359.3 17.3 %psum.59 = f32[32]{0:T(128)S(1)} all-reduce(f32[32]{0:T(128)S(1)} %multiply_reduce_fusion.3), channel_id=1, replica_groups=mesh['groups'=2,'brow'=8,'bcol'=2] {'brow'}, use_global_device_ids=true, to_apply=%region_16.17 | all-reduce | flops 32 | bytes 256 | tf_op jit(solution)/shard_map/psum | solution.py:158
  378.5 2.9 gather_fusion.6
  381.4 4.5 broadcast_multiply_fusion
  385.9 4.6 all-to-all-start.4
  392.6 17.3 %convolution_multiply_fusion.1 = f32[64,32,256]{2,1,0:T(8,128)} fusion(f32[64,32,256]{2,1,0:T(8,128)} %gather_fusion.8, f32[64,256,256]{2,1,0:T(8,128)} %bitcast.292, f32[64]{0:T(128)S(1)} %fusion.67), kind=kOutput, calls=%fused_computation.154 | convolution fusion | flops 1611137024 | bytes 20971776 | tf_op jit(solution)/shard_map/pab,pfa->pfb/dot_general | solution.py:130
  412.4 10.0 %scatter_fusion.1 = f32[128,32,256]{2,1,0:T(8,128)} fusion(f32[128,32,256]{2,1,0:T(8,128)} %broadcast.410, s32[64]{0:T(128)S(1)} %fusion.69, f32[64,32,256]{2,1,0:T(8,128)} %convolution_multiply_fusion.1), kind=kCustom, calls=%fused_computation.11 | custom fusion | bytes 6291712 | tf_op jit(solution)/shard_map/scatter | solution.py:134
  422.4 6.6 %copy.109 = f32[8,16,32,256]{3,1,2,0:T(8,128)} copy(f32[8,16,32,256]{3,2,1,0:T(8,128)} %bitcast.294) | data formatting | bytes 8388608 | tf_op jit(solution)/shard_map/reshape | solution.py:137
  428.9 48.4 %all-to-all-done.4 = f32[8,16,32,256]{3,2,1,0:T(8,128)} async-done(((f32[8,16,32,256]{3,2,1,0:T(8,128)}), f32[8,16,32,256]{3,2,1,0:T(8,128)}, u32[]{:S(2)}, u32[]{:S(2)}) %all-to-all-start.4) | async-done | bytes 4194336 | tf_op jit(solution)/shard_map/all_to_all | solution.py:126
  477.3 4.6 all-to-all-start.5
  482.2 4.3 gather_fusion.7
  486.5 23.1 %fusion.75 = f32[64,32,256]{2,1,0:T(8,128)} fusion(f32[64,32,256]{2,1,0:T(8,128)} %gather_fusion.7, f32[64,256,256]{2,1,0:T(8,128)} %bitcast.293), kind=kOutput, calls=%fused_computation.217 | convolution fusion | flops 1610612736 | bytes 20971520 | tf_op jit(solution)/shard_map/pab,pfb->pfa/dot_general | solution.py:128
  509.6 64.5 %all-to-all-done.5 = f32[8,16,32,256]{3,1,2,0:T(8,128)} async-done(((f32[8,16,32,256]{3,1,2,0:T(8,128)}), f32[8,16,32,256]{3,1,2,0:T(8,128)}, u32[]{:S(2)}, u32[]{:S(2)}) %all-to-all-start.5) | async-done | bytes 4194336 | tf_op jit(solution)/shard_map/all_to_all | solution.py:136
  578.6 3.1 fusion.50
  581.7 18.8 %all-reduce.6.cloned.1.call-done = f32[32,32,256]{2,0,1:T(8,128)} async-done(((f32[32,32,256]{2,0,1:T(8,128)}), f32[32,32,256]{2,0,1:T(8,128)}) %all-reduce.6.cloned.1.call-update) | async-done | bytes 1048592 | tf_op jit(solution)/shard_map/psum | solution.py:146
  602.6 21.6 %all-reduce = (f32[32]{0:T(128)S(1)}, f32[32]{0:T(128)S(1)}) all-reduce(f32[32]{0:T(128)S(1)} %get-tuple-element.244, f32[32]{0:T(128)S(1)} %get-tuple-element.243), channel_id=1, replica_groups=mesh['groups'=2,'brow'=8,'bcol'=2] {'brow'}, use_global_device_ids=true, to_apply=%region_22.23 | all-reduce | flops 64 | bytes 512 | tf_op jit(solution)/shard_map/psum | solution.py:161
  626.0 17.1 %psum.63 = f32[32]{0:T(128)S(1)} all-reduce(f32[32]{0:T(128)S(1)} %multiply_reduce_fusion), channel_id=1, replica_groups=mesh['groups'=2,'brow'=8,'bcol'=2] {'brow'}, use_global_device_ids=true, to_apply=%region_24.25 | all-reduce | flops 32 | bytes 256 | tf_op jit(solution)/shard_map/psum | solution.py:167
  (230 shorter events, 64.6 us)
Async XLA Ops:
  6.5 16.9 %copy-start = (f32[6,8192]{1,0:T(8,128)S(1)}, f32[6,8192]{1,0:T(8,128)}, u32[]{:S(2)}) copy-start(f32[6,8192]{1,0:T(8,128)} %param.19) | copy-start | bytes 589828
  23.3 2.0 copy-start.11
  23.3 35.8 %copy-start.9 = (f32[8,16]{1,0:T(8,128)}, f32[8,16]{1,0:T(8,128)S(1)}, u32[]{:S(2)}) copy-start(f32[8,16]{1,0:T(8,128)S(1)} %convert_bitcast_fusion) | copy-start | bytes 1540
  23.4 32.9 %copy-start.17 = (s32[1024]{0:T(1024)}, s32[1024]{0:T(1024)S(1)}, u32[]{:S(2)}) copy-start(s32[1024]{0:T(1024)S(1)} %pad_clamp_fusion.2) | copy-start | bytes 12292
  25.3 38.3 %all-to-all-start.2 = ((f32[8,16,6,256]{3,1,2,0:T(8,128)}), f32[8,16,6,256]{3,1,2,0:T(8,128)S(1)}, u32[]{:S(2)}, u32[]{:S(2)}) async-start(f32[8,16,6,256]{3,1,2,0:T(8,128)} %copy_multiply_fusion), calls=%async_computation.2 | async-start | bytes 1572864 | tf_op jit(solution)/shard_map/all_to_all | solution.py:113
  30.4 25.9 %copy-start.2 = (f32[4,8,32,256]{3,2,1,0:T(8,128)}, f32[4,8,32,256]{3,2,1,0:T(8,128)S(1)}, u32[]{:S(2)}) copy-start(f32[4,8,32,256]{3,2,1,0:T(8,128)S(1)} %copy.132) | copy-start | bytes 3145732
  55.5 0.8 copy-start.23
  55.5 0.8 copy-start.14
  63.6 116.5 %all-to-all-start.1 = ((f32[8,16,32,256]{3,2,1,0:T(8,128)}), f32[8,16,32,256]{3,2,1,0:T(8,128)}, u32[]{:S(2)}, u32[]{:S(2)}) async-start(f32[8,16,32,256]{3,2,1,0:T(8,128)} %broadcast_multiply_fusion.1), calls=%async_computation.1 | async-start | bytes 8388608 | tf_op jit(solution)/shard_map/all_to_all | solution.py:126
  68.4 2.7 copy-start.19
  69.0 2.1 copy-start.22
  69.1 2.2 copy-start.21
  71.1 1.2 copy-start.25
  71.1 1.2 copy-start.26
  71.2 1.1 copy-start.18
  180.1 39.7 %copy-start.12 = (s32[8,1,16]{2,1,0:T(1,128)S(1)}, s32[8,1,16]{2,1,0:T(1,128)}, u32[]{:S(2)}) copy-start(s32[8,1,16]{2,1,0:T(1,128)} %copy-done.11) | copy-start | bytes 1540
  180.1 129.5 %all-to-all-start.3 = ((f32[8,16,32,256]{3,1,2,0:T(8,128)}), f32[8,16,32,256]{3,1,2,0:T(8,128)}, u32[]{:S(2)}, u32[]{:S(2)}) async-start(f32[8,16,32,256]{3,1,2,0:T(8,128)} %copy.104), calls=%async_computation.3 | async-start | bytes 8388608 | tf_op jit(solution)/shard_map/all_to_all | solution.py:136
  219.3 115.9 %all-reduce.4.cloned.1.call-start = ((), (), s32[]{:S(2)}) async-start(), calls=%async_computation.6 | async-start | bytes 2097152 | tf_op jit(solution)/shard_map/psum | solution.py:146
  312.5 1.7 copy-start.8
  312.5 1.7 copy-start.20
  314.2 3.1 copy-start.13
  314.2 21.0 %copy-start.3 = (f32[4,8,32,256]{3,2,1,0:T(8,128)S(1)}, f32[4,8,32,256]{3,2,1,0:T(8,128)}, u32[]{:S(2)}) copy-start(f32[4,8,32,256]{3,2,1,0:T(8,128)} %copy-done.2) | copy-start | bytes 3145732
  314.2 21.0 %copy-start.15 = (f32[32]{0:T(128)S(1)}, f32[32]{0:T(128)}, u32[]{:S(2)}) copy-start(f32[32]{0:T(128)} %copy-done.14) | copy-start | bytes 388
  314.2 21.0 %copy-start.16 = (f32[32]{0:T(128)S(1)}, f32[32]{0:T(128)}, u32[]{:S(2)}) copy-start(f32[32]{0:T(128)} %param.21) | copy-start | bytes 388
  335.2 23.5 %copy-start.6 = (f32[32,32,256]{2,0,1:T(8,128)S(1)}, f32[32,32,256]{2,0,1:T(8,128)}, u32[]{:S(2)}) copy-start(f32[32,32,256]{2,0,1:T(8,128)} %all-reduce.4.cloned.1.call-done) | copy-start | bytes 3145732
  376.9 1.0 copy-start.4
  378.5 2.9 copy-start.10
  385.9 91.4 %all-to-all-start.4 = ((f32[8,16,32,256]{3,2,1,0:T(8,128)}), f32[8,16,32,256]{3,2,1,0:T(8,128)}, u32[]{:S(2)}, u32[]{:S(2)}) async-start(f32[8,16,32,256]{3,2,1,0:T(8,128)} %broadcast_multiply_fusion), calls=%async_computation.4 | async-start | bytes 8388608 | tf_op jit(solution)/shard_map/all_to_all | solution.py:126
  477.3 96.8 %all-to-all-start.5 = ((f32[8,16,32,256]{3,1,2,0:T(8,128)}), f32[8,16,32,256]{3,1,2,0:T(8,128)}, u32[]{:S(2)}, u32[]{:S(2)}) async-start(f32[8,16,32,256]{3,1,2,0:T(8,128)} %copy.109), calls=%async_computation.5 | async-start | bytes 8388608 | tf_op jit(solution)/shard_map/all_to_all | solution.py:136
  481.9 118.6 %all-reduce.6.cloned.1.call-start = ((), (), s32[]{:S(2)}) async-start(), calls=%async_computation.7 | async-start | bytes 2097152 | tf_op jit(solution)/shard_map/psum | solution.py:146
  576.9 1.7 copy-start.7
  578.6 21.9 %copy-start.5 = (f32[32,32,256]{2,0,1:T(8,128)S(1)}, f32[32,32,256]{2,0,1:T(8,128)}, u32[]{:S(2)}) copy-start(f32[32,32,256]{2,0,1:T(8,128)} %copy-done.4) | copy-start | bytes 3145732
  602.6 40.5 %copy-start.24 = (f32[32]{0:T(128)S(1)}, f32[32]{0:T(128)}, u32[]{:S(2)}) copy-start(f32[32]{0:T(128)} %copy-done.23) | copy-start | bytes 388
  643.2 1.8 copy-start.1
Sparse Core Ops, SparseCore 0:
  317.4 17.7 all-reduce.3
  581.8 18.6 all-reduce.5
where the time goes:
time: 657 us; the launch traced here: 652 us
  waiting for transfers between devices  215 us (33%)
  matrix products  135 us (21%)
  blocking collectives  116 us (18%)
  local copies, waits for them, and re-layouts  81.3 us (12%)
  starting transfers between devices  56.9 us (9%)
  other arithmetic  27.7 us (4%)
  between operations  14.3 us (2%)
    all_to_all x2, waiting for transfers between devices, apply_operator(): lax.all_to_all(send_back.reshape(owners, capacity, rhs_count, block_width...  130 us
    dot_general x8, matrix products, block_kernel(): jnp.einsum('gda,gdb->gab', left_geometry[:, 3:6, :], right_geometry[:, 3:...  48.4 us
    all_to_all x2, waiting for transfers between devices, apply_operator(): lax.all_to_all(give, 'brow', split_axis=0, concat_axis=0, tiled=True)  48.4 us
    all_to_all x2, starting transfers between devices, apply_operator(): lax.all_to_all(send_back.reshape(owners, capacity, rhs_count, block_width...  43.7 us
    dot_general x2, matrix products, apply_operator(): jnp.einsum('pab,pfb->pfa', blocks, column_vectors, precision=PRECISE)  43.3 us
    psum x2, waiting for transfers between devices, apply_operator(): near_sum = lax.psum(local_terms, 'bcol')  36.7 us
    dot_general x2, matrix products, apply_operator(): jnp.einsum('pab,pfa->pfb', blocks, row_vectors, precision=PRECISE)  30.8 us
    psum x1, blocking collectives, body(): start_norm = jnp.sqrt(lax.psum(product(start, start), 'brow') + EPSILON)  24.7 us
  transfers between devices with their start and end apart: 7, of which 5 were waited for; matrix products, arithmetic and copies ran while one was open for 32% of the time, Pallas kernels for 0%

commit v1 on v0

--- a/solution.py
+++ b/solution.py
@@ -4,6 +4,8 @@
 import jax
 import jax.numpy as jnp
 from jax import lax
+from jax.experimental import pallas as pl
+from jax.experimental.pallas import tpu as pltpu
 from jax.sharding import PartitionSpec as P
 
 BS = 256
@@ -75,7 +77,7 @@
     return assembled.reshape(total_pairs, block_width, block_width)
 
 
-def body(near_pairs, rule_orders, geometry, resist, laplace, right_sides):
+def plain_body(near_pairs, rule_orders, geometry, resist, laplace, right_sides):
     owners = lax.axis_size("brow")
     here = lax.axis_index("brow")
     block_width = BS
@@ -177,6 +179,502 @@
     return combined.transpose(1, 0, 2).reshape(rhs_count, blocks_here * block_width)
 
 
+MESH = pl.DeviceIdType.MESH
+LIMIT = 56 * 1024 * 1024
+NODES = ((0.0,), (-GAUSS_TWO, GAUSS_TWO), (-GAUSS_THREE, 0.0, GAUSS_THREE))
+WEIGHTS = ((1.0,), (0.5, 0.5), (5.0 / 18.0, 8.0 / 18.0, 5.0 / 18.0))
+
+
+def ring_place(brow, count):
+    return brow // 2 + (brow % 2) * (count - 1 - 2 * (brow // 2))
+
+
+def ring_owner(place, count):
+    upper = place // (count // 2)
+    return 2 * place + upper * (2 * (count - 1 - place) + 1 - 2 * place)
+
+
+def gather_kernel(count, mine_ref, all_ref, own_sem, send_sem, recv_sem, give_sem, take_sem):
+    brow, core = lax.axis_index("brow"), lax.axis_index("bcol")
+    groups = lax.axis_index("groups")
+    place = ring_place(brow, count)
+    ahead = ring_owner((place + 1) % count, count)
+    behind = ring_owner((place + count - 1) % count, count)
+    targets = ((groups, ahead, core), (groups, behind, core))
+    other = (groups, brow, 1 - core)
+    part = mine_ref.shape[0] // 2
+    barrier = pltpu.get_barrier_semaphore()
+    for device in targets + (other,):
+        pl.semaphore_signal(barrier, inc=1, device_id=device, device_id_type=MESH)
+    pl.semaphore_wait(barrier, 3)
+
+    def piece(owner, half):
+        return all_ref.at[2 * owner + core, pl.ds(half * part, part)]
+
+    last = count - 2
+
+    def half_of(way, index):
+        return (index % 2) if way == 0 else 1 - index % 2
+
+    def owner_of(way, steps):
+        shift = count - steps if way == 0 else steps
+        return ring_owner((place + shift) % count, count)
+
+    def ring_copy(way, index):
+        step, half = index // 2, half_of(way, index)
+        owner = owner_of(way, step) if step else brow
+        source = piece(owner, half) if step else mine_ref.at[pl.ds(half * part, part)]
+        return pltpu.make_async_remote_copy(
+            src_ref=source,
+            dst_ref=piece(owner, half),
+            send_sem=send_sem.at[way, index],
+            recv_sem=recv_sem.at[way, index],
+            device_id=targets[way],
+            device_id_type=MESH,
+        )
+
+    def landing(way, index):
+        owner, half = owner_of(way, index // 2 + 1), half_of(way, index)
+        return pltpu.make_async_remote_copy(
+            src_ref=piece(owner, half),
+            dst_ref=piece(owner, half),
+            send_sem=send_sem.at[way, index],
+            recv_sem=recv_sem.at[way, index],
+            device_id=targets[way],
+            device_id_type=MESH,
+        )
+
+    def core_copy(number, source, target):
+        return pltpu.make_async_remote_copy(
+            src_ref=source,
+            dst_ref=target,
+            send_sem=give_sem.at[number],
+            recv_sem=take_sem.at[number],
+            device_id=other,
+            device_id_type=MESH,
+        )
+
+    own = pltpu.make_async_copy(mine_ref, all_ref.at[2 * brow + core], own_sem)
+    own.start()
+    sends, gives = [], []
+    for index in range(2):
+        for way in range(2):
+            copy = ring_copy(way, index)
+            copy.start()
+            sends.append(copy)
+    copy = core_copy(0, mine_ref, all_ref.at[2 * brow + core])
+    copy.start()
+    gives.append(copy)
+    for index in range(last + 1):
+        for way in range(2):
+            landing(way, index).wait_recv()
+            if index + 2 <= last:
+                copy = ring_copy(way, index + 2)
+                copy.start()
+                sends.append(copy)
+            view = piece(owner_of(way, index // 2 + 1), half_of(way, index))
+            copy = core_copy(1 + 2 * index + way, view, view)
+            copy.start()
+            gives.append(copy)
+    own.wait()
+    for copy in sends:
+        copy.wait_send()
+    for number, copy in enumerate(gives):
+        copy.wait_send()
+        if number == 0:
+            target = all_ref.at[2 * brow + 1 - core]
+        else:
+            way, index = (number - 1) % 2, (number - 1) // 2
+            owner, half = owner_of(way, index // 2 + 1), half_of(way, index)
+            target = all_ref.at[2 * owner + 1 - core, pl.ds(half * part, part)]
+        core_copy(number, target, target).wait_recv()
+
+
+def gather_all(mine, count, number):
+    pieces = 2 * (count - 1)
+    return pl.pallas_call(
+        partial(gather_kernel, count),
+        out_shape=jax.ShapeDtypeStruct((2 * count,) + mine.shape, mine.dtype),
+        in_specs=[pl.BlockSpec(memory_space=pl.ANY)],
+        out_specs=pl.BlockSpec(memory_space=pl.ANY),
+        scratch_shapes=[
+            pltpu.SemaphoreType.DMA,
+            pltpu.SemaphoreType.DMA((2, count - 1)),
+            pltpu.SemaphoreType.DMA((2, count - 1)),
+            pltpu.SemaphoreType.DMA((1 + pieces,)),
+            pltpu.SemaphoreType.DMA((1 + pieces,)),
+        ],
+        compiler_params=pltpu.CompilerParams(collective_id=number, has_side_effects=True),
+        name="gather_all",
+    )(mine)
+
+
+def sum_kernel(count, part_ref, sum_ref, inbox, send_sem, recv_sem):
+    brow, core = lax.axis_index("brow"), lax.axis_index("bcol")
+    groups = lax.axis_index("groups")
+    here = 2 * brow + core
+    total = 2 * count
+    barrier = pltpu.get_barrier_semaphore()
+    devices = []
+    for shift in range(1, total):
+        index = (here + shift) % total
+        devices.append((groups, index // 2, index % 2))
+    for device in devices:
+        pl.semaphore_signal(barrier, inc=1, device_id=device, device_id_type=MESH)
+    pl.semaphore_wait(barrier, total - 1)
+    copies = []
+    for shift, device in enumerate(devices):
+        copy = pltpu.make_async_remote_copy(
+            src_ref=part_ref,
+            dst_ref=inbox.at[shift],
+            send_sem=send_sem.at[shift],
+            recv_sem=recv_sem.at[shift],
+            device_id=device,
+            device_id_type=MESH,
+        )
+        copy.start()
+        copies.append(copy)
+    for copy in copies:
+        copy.wait()
+    slots = [part_ref[...]] + [inbox[shift] for shift in range(total - 1)]
+    result = jnp.zeros_like(slots[0])
+    for index in range(total):
+        term = jnp.zeros_like(result)
+        for shift in range(total):
+            source = (here + total - shift) % total
+            term = term + jnp.where(source == index, slots[shift], 0.0)
+        result = result + term
+    sum_ref[...] = result
+
+
+def sum_all(part, count, number):
+    total = 2 * count
+    return pl.pallas_call(
+        partial(sum_kernel, count),
+        out_shape=jax.ShapeDtypeStruct(part.shape, part.dtype),
+        in_specs=[pl.BlockSpec(memory_space=pltpu.VMEM)],
+        out_specs=pl.BlockSpec(memory_space=pltpu.VMEM),
+        scratch_shapes=[
+            pltpu.VMEM((total - 1,) + part.shape, part.dtype),
+            pltpu.SemaphoreType.DMA((total - 1,)),
+            pltpu.SemaphoreType.DMA((total - 1,)),
+        ],
+        compiler_params=pltpu.CompilerParams(collective_id=number, has_side_effects=True),
+        name="sum_all",
+    )(part)
+
+
+def swap_kernel(mine_ref, both_ref, own_sem, send_sem, recv_sem):
+    brow, core = lax.axis_index("brow"), lax.axis_index("bcol")
+    other = (lax.axis_index("groups"), brow, 1 - core)
+    barrier = pltpu.get_barrier_semaphore()
+    pl.semaphore_signal(barrier, inc=1, device_id=other, device_id_type=MESH)
+    pl.semaphore_wait(barrier, 1)
+    copy = pltpu.make_async_remote_copy(
+        src_ref=mine_ref,
+        dst_ref=both_ref.at[core],
+        send_sem=send_sem,
+        recv_sem=recv_sem,
+        device_id=other,
+        device_id_type=MESH,
+    )
+    copy.start()
+    own = pltpu.make_async_copy(mine_ref, both_ref.at[core], own_sem)
+    own.start()
+    own.wait()
+    copy.wait()
+
+
+def swap_cores(mine, number):
+    return pl.pallas_call(
+        swap_kernel,
+        out_shape=jax.ShapeDtypeStruct((2,) + mine.shape, mine.dtype),
+        in_specs=[pl.BlockSpec(memory_space=pl.ANY)],
+        out_specs=pl.BlockSpec(memory_space=pl.ANY),
+        scratch_shapes=[pltpu.SemaphoreType.DMA] * 3,
+        compiler_params=pltpu.CompilerParams(collective_id=number, has_side_effects=True),
+        name="swap_cores",
+    )(mine)
+
+
+def multiply(vector, block_ref):
+    width = block_ref.shape[1]
+    coarse = vector.astype(jnp.bfloat16)
+    fine = (vector - coarse.astype(jnp.float32)).astype(jnp.bfloat16)
+    rows = vector.shape[0]
+    both = jnp.dot(
+        jnp.concatenate([coarse, fine], axis=0),
+        block_ref[0:width, :],
+        preferred_element_type=jnp.float32,
+    )
+    rest = jnp.dot(coarse, block_ref[width : 2 * width, :], preferred_element_type=jnp.float32)
+    return both[:rows] + (both[rows:] + rest)
+
+
+def build_kernel(first_row, count_ref, source_ref, target_ref, place_ref, order_ref, all_ref, near_ref, blocks_ref, buffer, sems):
+    width = near_ref.shape[2]
+    rows = near_ref.shape[1]
+    near_ref[...] = jnp.zeros_like(near_ref)
+    total = count_ref[0]
+    tile = 64
+
+    def copy_out(slot, edge):
+        return pltpu.make_async_copy(buffer.at[slot], blocks_ref.at[edge], sems.at[slot])
+
+    def one_edge(edge, carry):
+        slot = lax.rem(edge, 2)
+
+        @pl.when(edge >= 2)
+        def _():
+            copy_out(slot, edge - 2).wait()
+
+        source, target, order = source_ref[edge], target_ref[edge], order_ref[edge]
+        left = all_ref[source, rows : rows + 8, :]
+        right = all_ref[target, rows : rows + 8, :]
+        tangent_left = jnp.transpose(left)
+
+        for level in range(3):
+            nodes, weights = NODES[level], WEIGHTS[level]
+
+            @pl.when(order == level + 1)
+            def _():
+                columns = []
+                lines = []
+                for node in nodes:
+                    if node == 0.0:
+                        columns.append(tangent_left)
+                        lines.append(right[0:3])
+                    else:
+                        moved = left[0:3] + node * left[3:6]
+                        columns.append(
+                            jnp.transpose(jnp.concatenate([moved, left[3:8]], axis=0))
+                        )
+                        lines.append(right[0:3] + node * right[3:6])
+                for start in range(0, width, tile):
+                    part = slice(start, start + tile)
+                    classes = {}
+                    for m in range(len(nodes)):
+                        for n in range(len(nodes)):
+                            squared = None
+                            for component in range(3):
+                                offset = (
+                                    columns[m][part, component : component + 1]
+                                    - lines[n][component : component + 1, :]
+                                )
+                                term = offset * offset
+                                squared = term + RADIUS_SQUARED if squared is None else squared + term
+                            value = lax.rsqrt(squared)
+                            weight = weights[m] * weights[n]
+                            classes[weight] = (
+                                classes[weight] + value if weight in classes else value
+                            )
+                    summed = None
+                    for weight, value in classes.items():
+                        value = value if weight == 1.0 else weight * value
+                        summed = value if summed is None else summed + value
+                    dots = None
+                    for component in range(3, 6):
+                        term = (
+                            tangent_left[part, component : component + 1]
+                            * right[component : component + 1, :]
+                        )
+                        dots = term if dots is None else dots + term
+                    block = dots * summed
+                    coarse = block.astype(jnp.bfloat16)
+                    fine = (block - coarse.astype(jnp.float32)).astype(jnp.bfloat16)
+                    buffer[slot, start : start + tile, :] = coarse
+                    buffer[slot, width + start : width + start + tile, :] = fine
+
+        copy_out(slot, edge).start()
+        place = place_ref[edge]
+        near_ref[place] = near_ref[place] + multiply(all_ref[source, 0:rows, :], buffer.at[slot])
+        return carry
+
+    lax.fori_loop(0, total, one_edge, 0)
+
+    @pl.when(total >= 2)
+    def _():
+        copy_out(lax.rem(total, 2), total - 2).wait()
+
+    @pl.when(total >= 1)
+    def _():
+        copy_out(lax.rem(total + 1, 2), total - 1).wait()
+
+
+DEPTH = 4
+
+
+def apply_kernel(count_ref, source_ref, place_ref, all_ref, blocks_ref, near_ref, buffer, sems):
+    near_ref[...] = jnp.zeros_like(near_ref)
+    total = count_ref[0]
+
+    def copy_in(edge):
+        slot = lax.rem(edge, DEPTH)
+        return pltpu.make_async_copy(blocks_ref.at[edge], buffer.at[slot], sems.at[slot])
+
+    for edge in range(DEPTH - 1):
+
+        @pl.when(edge < total)
+        def _():
+            copy_in(jnp.int32(edge)).start()
+
+    def one_edge(edge, carry):
+        @pl.when(edge + DEPTH - 1 < total)
+        def _():
+            copy_in(edge + DEPTH - 1).start()
+
+        copy_in(edge).wait()
+        place = place_ref[edge]
+        slot = lax.rem(edge, DEPTH)
+        near_ref[place] = near_ref[place] + multiply(all_ref[source_ref[edge]], buffer.at[slot])
+        return carry
+
+    lax.fori_loop(0, total, one_edge, 0)
+
+
+def edge_list(near_pairs, rule_orders, me, half, room):
+    row, column = near_pairs[:, 0], near_pairs[:, 1]
+    source = jnp.concatenate([column, row])
+    target = jnp.concatenate([row, column])
+    order = jnp.concatenate([rule_orders, rule_orders])
+    mine = target // half == me
+    mine = mine & jnp.concatenate([jnp.ones(row.shape, bool), row != column])
+    lanes = 128
+    grid = mine.astype(jnp.float32).reshape(-1, lanes)
+    upper = jnp.triu(jnp.ones((lanes, lanes), jnp.float32), 1)
+    lower = jnp.tril(jnp.ones((grid.shape[0], grid.shape[0]), jnp.float32), -1)
+    inside = jnp.dot(grid, upper, precision=PRECISE)
+    before = jnp.dot(lower, jnp.sum(grid, axis=1, keepdims=True), precision=PRECISE)
+    position = (inside + before).reshape(-1).astype(jnp.int32)
+    position = jnp.where(mine, position, -1)
+    code = (source * half + target % half) * 4 + order
+    hit = position[None, :] == jnp.arange(room, dtype=jnp.int32)[:, None]
+    picked = jnp.sum(jnp.where(hit, code[None, :], 0), axis=1)
+    count = jnp.sum(mine.astype(jnp.int32)).reshape(1)
+    order = picked % 4
+    place = picked // 4 % half
+    return count, picked // (4 * half), me * half + place, place, order
+
+
+def gather_body(near_pairs, rule_orders, geometry, resist, laplace, right_sides):
+    owners = lax.axis_size("brow")
+    halves = lax.axis_size("bcol")
+    core = lax.axis_index("bcol")
+    me = lax.axis_index("brow") * halves + core
+    width = BS
+    blocks_here = geometry.shape[1] // width
+    half = blocks_here // halves
+    all_blocks = owners * blocks_here
+    rhs_count = right_sides.shape[0]
+    pair_count = near_pairs.shape[0]
+    capacity = max(2, 2 * pair_count // owners)
+    room = halves * pair_count + halves * owners * capacity
+
+    listed = lax.all_gather(
+        jnp.concatenate([near_pairs, rule_orders[:, None]], axis=1),
+        ("brow", "bcol"),
+        axis=0,
+        tiled=True,
+    )
+    count, source, target, place, order = edge_list(listed[:, 0:2], listed[:, 2], me, half, room)
+
+    def own_half(array):
+        rows = array.shape[0]
+        part = lax.dynamic_slice_in_dim(array, core * half * width, half * width, 1)
+        return part.reshape(rows, half, width).transpose(1, 0, 2)
+
+    start = own_half(right_sides)
+    shape_own = own_half(geometry)
+    mine = jnp.concatenate([start, shape_own, jnp.zeros((half, 2, width), jnp.float32)], axis=1)
+    everything = gather_all(mine, owners, 0).reshape(all_blocks, rhs_count + 8, width)
+    smem = pl.BlockSpec(memory_space=pltpu.SMEM)
+    vmem = pl.BlockSpec(memory_space=pltpu.VMEM)
+    hbm = pl.BlockSpec(memory_space=pl.ANY)
+    near_shape = jax.ShapeDtypeStruct((half, rhs_count, width), jnp.float32)
+    near_start, blocks = pl.pallas_call(
+        partial(build_kernel, 0),
+        out_shape=(near_shape, jax.ShapeDtypeStruct((room, 2 * width, width), jnp.bfloat16)),
+        in_specs=[smem] * 5 + [vmem],
+        out_specs=(vmem, hbm),
+        scratch_shapes=[
+            pltpu.VMEM((2, 2 * width, width), jnp.bfloat16),
+            pltpu.SemaphoreType.DMA((2,)),
+        ],
+        compiler_params=pltpu.CompilerParams(vmem_limit_bytes=LIMIT),
+        name="build_blocks",
+    )(count, source, target, place, order, everything)
+
+    resist_own = lax.dynamic_slice_in_dim(resist, core * half * width, half * width, 0).reshape(
+        half, 1, width
+    )
+    laplace_rows = laplace.reshape(1, rhs_count, 1)
+
+    def spread(amount):
+        return amount[None, :, None]
+
+    def dots(number, *couples):
+        parts = [jnp.sum(left * right, axis=(0, 2)) for left, right in couples]
+        packed = jnp.zeros((8, 128), jnp.float32)
+        packed = packed.at[0 : len(parts), 0:rhs_count].set(jnp.stack(parts))
+        total = sum_all(packed, owners, number)
+        return [total[row, 0:rhs_count] for row in range(len(parts))]
+
+    image = resist_own * start + laplace_rows * near_start
+    everything_two = gather_all(image, owners, 1).reshape(all_blocks, rhs_count, width)
+    near_image = pl.pallas_call(
+        apply_kernel,
+        out_shape=near_shape,
+        in_specs=[smem] * 3 + [vmem, hbm],
+        out_specs=vmem,
+        scratch_shapes=[
+            pltpu.VMEM((DEPTH, 2 * width, width), jnp.bfloat16),
+            pltpu.SemaphoreType.DMA((DEPTH,)),
+        ],
+        compiler_params=pltpu.CompilerParams(vmem_limit_bytes=LIMIT),
+        name="apply_blocks",
+    )(count, source, place, everything_two, blocks)
+
+    start_square, start_image = dots(2, (start, start), (start, image))
+    start_norm = jnp.sqrt(start_square + EPSILON)
+    first = start / spread(start_norm)
+    along_first = start_image / start_norm / start_norm
+    second_raw = image / spread(start_norm) - spread(along_first) * first
+    (rest_square,) = dots(3, (second_raw, second_raw))
+    rest_first = jnp.sqrt(rest_square + EPSILON)
+    second = second_raw / spread(rest_first)
+    near_second = (
+        (near_image - spread(along_first) * near_start) / spread(start_norm) / spread(rest_first)
+    )
+    image_two = resist_own * second + laplace_rows * near_second
+    along_cross, along_second = dots(4, (first, image_two), (second, image_two))
+    remainder = image_two - spread(along_cross) * first - spread(along_second) * second
+    (last_square,) = dots(5, (remainder, remainder))
+    rest_second = jnp.sqrt(last_square + EPSILON)
+    radius_one = jnp.sqrt(along_first * along_first + rest_first * rest_first)
+    cosine_one = along_first / radius_one
+    sine_one = rest_first / radius_one
+    upper_right = cosine_one * along_cross + sine_one * along_second
+    lower_right = cosine_one * along_second - sine_one * along_cross
+    radius_two = jnp.sqrt(lower_right * lower_right + rest_second * rest_second)
+    amount_two = -(lower_right / radius_two) * start_norm * sine_one / radius_two
+    amount_one = (start_norm * cosine_one - upper_right * amount_two) / radius_one
+    combined = spread(amount_one) * first + spread(amount_two) * second
+    return (
+        swap_cores(combined, 6)
+        .reshape(blocks_here, rhs_count, width)
+        .transpose(1, 0, 2)
+        .reshape(rhs_count, blocks_here * width)
+    )
+
+
+def body(near_pairs, rule_orders, geometry, resist, laplace, right_sides):
+    owners = lax.axis_size("brow")
+    blocks = geometry.shape[1] // BS * owners
+    if owners == 8 and lax.axis_size("bcol") == 2 and blocks <= 256:
+        return gather_body(near_pairs, rule_orders, geometry, resist, laplace, right_sides)
+    return plain_body(near_pairs, rule_orders, geometry, resist, laplace, right_sides)
+
+
 def solution(mesh):
     return jax.shard_map(
         body,

time: 657 us -> 380 us (0.58)
  Pallas kernels: 0 us -> 336 us
  waiting for transfers between devices: 215 us -> 0 us
  matrix products: 135 us -> 0.31 us
  blocking collectives: 116 us -> 23.1 us
  local copies, waits for them, and re-layouts: 81.3 us -> 5.45 us
  starting transfers between devices: 56.9 us -> 0 us
  between operations: 14.3 us -> 0.19 us
  other arithmetic: 27.7 us -> 13.7 us
    pallas_call x0 -> x9, Pallas kernels: none -> 336 us  [the longest x1 121 us: gather_body(): pl.pallas_call(partial(build_kernel, 0), out_shape=(near_shape, jax.Shape...]
    all_to_all x5 -> x0, waiting for transfers between devices: 179 us -> none  [the longest x2 130 us: apply_operator(): lax.all_to_all(send_back.reshape(owners, capacity, rhs_count, block_width...]
    dot_general x32 -> x2, matrix products: 135 us -> 0.31 us  [the longest x1 0.2 us: edge_list(): jnp.dot(lower, jnp.sum(grid, axis=1, keepdims=True), precision=PRECISE)]
    psum x5 -> x0, blocking collectives: 102 us -> none  [the longest x1 24.7 us: body(): start_norm = jnp.sqrt(lax.psum(product(start, start), 'brow') + EPSILON)]
    all_to_all x5 -> x0, starting transfers between devices: 56.6 us -> none  [the longest x2 43.7 us: apply_operator(): lax.all_to_all(send_back.reshape(owners, capacity, rhs_count, block_width...]
    psum x2 -> x0, waiting for transfers between devices: 36.7 us -> none  [apply_operator(): near_sum = lax.psum(local_terms, 'bcol')]
    all_gather x0 -> x1, blocking collectives: none -> 23.1 us  [gather_body(): lax.all_gather(jnp.concatenate([near_pairs, rule_orders[:, None]], axis=1...]
    gather x9 -> x0, local copies, waits for them, and re-layouts: 19.2 us -> none  [the longest x2 7.32 us: apply_operator(): fetched.reshape(slot_count, rhs_count, block_width)[slot_of]]
  transfers between devices with their start and end apart: 7 -> 0, of which waited for: 5 -> 0; matrix products, arithmetic and copies ran while one was open for 32% -> 0% of each run, Pallas kernels for 0% -> 0%
where the time goes in v1:
time: 380 us; the launch traced here: 379 us
  Pallas kernels  336 us (88%)
  blocking collectives  23.1 us (6%)
  other arithmetic  13.7 us (4%)
  local copies, waits for them, and re-layouts  5.45 us (1%)
    pallas_call x1, Pallas kernels, gather_body(): pl.pallas_call(partial(build_kernel, 0), out_shape=(near_shape, jax.Shape...  121 us
    pallas_call x2, Pallas kernels, gather_all(): pl.pallas_call(partial(gather_kernel, count), out_shape=jax.ShapeDtypeStr...  115 us
    pallas_call x1, Pallas kernels, gather_body(): pl.pallas_call(apply_kernel, out_shape=near_shape, in_specs=[smem] * 3 +...  45.2 us
    pallas_call x4, Pallas kernels, sum_all(): pl.pallas_call(partial(sum_kernel, count), out_shape=jax.ShapeDtypeStruct...  38.1 us
    all_gather x1, blocking collectives, gather_body(): lax.all_gather(jnp.concatenate([near_pairs, rule_orders[:, None]], axis=1...  23.1 us
    pallas_call x1, Pallas kernels, swap_cores(): pl.pallas_call(swap_kernel, out_shape=jax.ShapeDtypeStruct((2,) + mine.sh...  17.1 us

profile of v1, /device:TPU:0, one launch (start us, length us, event | category | flops | bytes accessed | tf_op | source)
XLA Modules:
  0.0 378.8 jit_solution(13921571944550955569)
XLA Ops:
  0.0 0.0 copy-start
  0.0 0.8 add_bitcast_fusion
  0.8 23.1 %all-gather = s32[16,64,3]{1,2,0:T(4,128)S(1)} all-gather(s32[1,64,3]{1,2,0:T(4,128)S(1)} %add_bitcast_fusion), channel_id=1, replica_groups=mesh['groups'=2,'brow'=8,'bcol'=2] {'brow','bcol'}, dimensions={0}, use_global_device_ids=true | all-gather | bytes 13056 | tf_op jit(solution)/shard_map/all_gather | solution.py:573
  23.9 0.1 reshape.359
  24.0 0.1 convert_reduce_fusion
  24.2 0.2 convolution_bitcast_fusion
  24.4 0.1 fusion.2
  24.5 0.1 fusion.9
  24.6 0.4 select_reduce_fusion
  25.0 0.6 broadcast_add_fusion
  25.6 0.0 copy-done
  25.7 0.9 constant_dynamic-slice_fusion
  26.6 0.1 pad.28.clone
  26.7 1.0 maximum_maximum_fusion.mine_ref
  27.6 55.0 %gather_all.2 = f32[16,16,40,256]{3,2,1,0:T(8,128)} custom-call(f32[16,40,256]{2,1,0:T(8,128)} %maximum_maximum_fusion.mine_ref), custom_call_target="tpu_custom_call" | custom-call | tf_op jit(solution)/shard_map/gather_all/pallas_call | solution.py:295
  82.6 0.7 convert_reduce_fusion.1
  83.3 0.0 dynamic-slice-start
  83.3 0.0 copy-start.3
  83.3 120.9 %build_blocks.1 = (f32[16,32,256]{2,1,0:T(8,128)}, bf16[384,512,256]{2,1,0:T(8,128)(2,1)}) custom-call(s32[1]{0:T(128)} %bitcast.6.count_ref, s32[384]{0:T(512)} %get-tuple-element.79.source_ref, s32[384]{0:T(512)} %get-tuple-element.67.target_ref, s32[384]{0:T(512)} %get-tuple-element.68.place_ref, s32[384]{0:T(512)} %get-tuple-element.78.order_ref, ...), custom_call_target="tpu_custom_call" | custom-call | tf_op jit(solution)/shard_map/build_blocks/pallas_call | solution.py:594
  204.3 0.0 dynamic-slice-done
  204.3 0.0 copy-done.3
  204.3 2.1 multiply_reduce_fusion.5
  206.4 59.7 %gather_all.3 = f32[16,16,32,256]{3,2,1,0:T(8,128)} custom-call(f32[16,32,256]{2,1,0:T(8,128)} %get-tuple-element.66.mine_ref), custom_call_target="tpu_custom_call" | custom-call | tf_op jit(solution)/shard_map/gather_all/pallas_call | solution.py:295
  266.1 0.0 copy-start.1
  266.1 0.0 copy-start.2
  266.1 45.2 %apply_blocks.1 = f32[16,32,256]{2,1,0:T(8,128)} custom-call(s32[1]{0:T(128)} %bitcast.6.count_ref, s32[384]{0:T(512)} %get-tuple-element.79.source_ref, s32[384]{0:T(512)} %get-tuple-element.68.place_ref, f32[256,32,256]{2,1,0:T(8,128)} %bitcast.138, bf16[384,512,256]{2,1,0:T(8,128)(2,1)} %get-tuple-element.56.blocks_ref), custom_call_target="tpu_custom_call" | custom-call | tf_op jit(solution)/shard_map/apply_blocks/pallas_call | solution.py:624
  311.4 0.6 select_maximum_fusion.1.part_ref
  312.0 13.3 %sum_all.4 = f32[8,128]{1,0:T(8,128)} custom-call(f32[8,128]{1,0:T(8,128)} %select_maximum_fusion.1.part_ref), custom_call_target="tpu_custom_call" | custom-call | tf_op jit(solution)/shard_map/sum_all/pallas_call | solution.py:352
  325.3 0.8 bitcast_divide_fusion.1
  326.1 0.7 sqrt_bitcast_fusion.1
  326.8 0.0 copy-done.1
  326.8 0.3 multiply_reduce_fusion.3
  327.1 0.6 scatter.15.part_ref
  327.7 8.2 %sum_all.5 = f32[8,128]{1,0:T(8,128)} custom-call(f32[8,128]{1,0:T(8,128)} %scatter.15.part_ref), custom_call_target="tpu_custom_call" | custom-call | tf_op jit(solution)/shard_map/sum_all/pallas_call | solution.py:352
  335.9 0.8 fusion.27
  336.7 0.7 sqrt_bitcast_fusion
  337.4 0.0 copy-done.2
  337.4 1.4 multiply_reduce_fusion.2
  338.8 0.6 select_maximum_fusion.part_ref
  339.4 8.3 %sum_all.6 = f32[8,128]{1,0:T(8,128)} custom-call(f32[8,128]{1,0:T(8,128)} %select_maximum_fusion.part_ref), custom_call_target="tpu_custom_call" | custom-call | tf_op jit(solution)/shard_map/sum_all/pallas_call | solution.py:352
  347.7 0.8 slice_bitcast_fusion.1
  348.4 0.3 multiply_reduce_fusion
  348.8 0.6 scatter.19.part_ref
  349.4 8.3 %sum_all.7 = f32[8,128]{1,0:T(8,128)} custom-call(f32[8,128]{1,0:T(8,128)} %scatter.19.part_ref), custom_call_target="tpu_custom_call" | custom-call | tf_op jit(solution)/shard_map/sum_all/pallas_call | solution.py:352
  357.6 0.8 subtract_divide_fusion
  358.5 1.0 multiply_add_fusion.mine_ref
  359.4 17.1 %swap_cores.1 = f32[2,16,32,256]{3,2,1,0:T(8,128)} custom-call(f32[16,32,256]{2,1,0:T(8,128)} %multiply_add_fusion.mine_ref), custom_call_target="tpu_custom_call" | custom-call | tf_op jit(solution)/shard_map/swap_cores/pallas_call | solution.py:389
  376.5 2.3 copy.18
  (8 shorter events, 0.1 us)
Async XLA Ops:
  0.0 25.6 %copy-start = (f32[32,8192]{1,0:T(8,128)S(1)}, f32[32,8192]{1,0:T(8,128)}, u32[]{:S(2)}) copy-start(f32[32,8192]{1,0:T(8,128)} %param.19) | copy-start | bytes 3145732
  83.3 120.9 %dynamic-slice-start = ((f32[8192]{0:T(1024)}, s32[]{:T(128)}), f32[4096]{0:T(1024)S(1)}, s32[]{:S(2)}) async-start(f32[8192]{0:T(1024)} %param.17, s32[]{:T(128)} %select_n.55), calls=%async_computation | async-start | bytes 33280 | tf_op jit(solution)/shard_map/dynamic_slice | solution.py:607
  83.3 121.0 %copy-start.3 = (f32[32]{0:T(128)S(1)}, f32[32]{0:T(128)}, u32[]{:S(2)}) copy-start(f32[32]{0:T(128)} %param.18) | copy-start | bytes 388
  266.1 60.7 %copy-start.1 = (f32[16,32,256]{2,1,0:T(8,128)S(1)}, f32[16,32,256]{2,1,0:T(8,128)}, u32[]{:S(2)}) copy-start(f32[16,32,256]{2,1,0:T(8,128)} %get-tuple-element.66.mine_ref) | copy-start | bytes 1572868
  266.1 71.3 %copy-start.2 = (f32[16,32,256]{2,1,0:T(8,128)S(1)}, f32[16,32,256]{2,1,0:T(8,128)}, u32[]{:S(2)}) copy-start(f32[16,32,256]{2,1,0:T(8,128)} %get-tuple-element.55) | copy-start | bytes 1572868

commit v2 on v1

--- a/solution.py
+++ b/solution.py
@@ -309,92 +309,142 @@
     )(mine)
 
 
-def sum_kernel(count, part_ref, sum_ref, inbox, send_sem, recv_sem):
+def finish_kernel(
+    count, start_ref, image_ref, near_start_ref, near_image_ref, resist_ref, laplace_ref,
+    amounts_ref, outbox, inbox, kept, send_sem, recv_sem,
+):
     brow, core = lax.axis_index("brow"), lax.axis_index("bcol")
     groups = lax.axis_index("groups")
     here = 2 * brow + core
     total = 2 * count
-    barrier = pltpu.get_barrier_semaphore()
-    devices = []
+    blocks, rhs, width = start_ref.shape
+    others = []
     for shift in range(1, total):
         index = (here + shift) % total
-        devices.append((groups, index // 2, index % 2))
-    for device in devices:
+        others.append((index, (groups, index // 2, index % 2)))
+    barrier = pltpu.get_barrier_semaphore()
+    for index, device in others:
         pl.semaphore_signal(barrier, inc=1, device_id=device, device_id_type=MESH)
-    pl.semaphore_wait(barrier, total - 1)
-    copies = []
-    for shift, device in enumerate(devices):
-        copy = pltpu.make_async_remote_copy(
-            src_ref=part_ref,
-            dst_ref=inbox.at[shift],
-            send_sem=send_sem.at[shift],
-            recv_sem=recv_sem.at[shift],
-            device_id=device,
-            device_id_type=MESH,
-        )
-        copy.start()
-        copies.append(copy)
-    for copy in copies:
-        copy.wait()
-    slots = [part_ref[...]] + [inbox[shift] for shift in range(total - 1)]
-    result = jnp.zeros_like(slots[0])
-    for index in range(total):
-        term = jnp.zeros_like(result)
-        for shift in range(total):
-            source = (here + total - shift) % total
-            term = term + jnp.where(source == index, slots[shift], 0.0)
-        result = result + term
-    sum_ref[...] = result
-
-
-def sum_all(part, count, number):
+    outbox[...] = jnp.zeros_like(outbox)
+    diagonal = lax.broadcasted_iota(jnp.int32, (rhs, rhs), 0) == lax.broadcasted_iota(
+        jnp.int32, (rhs, rhs), 1
+    )
+
+    def to_row(column):
+        return jnp.sum(jnp.where(diagonal, column, 0.0), axis=0, keepdims=True)
+
+    def to_column(row):
+        return jnp.sum(jnp.where(diagonal, row, 0.0), axis=1, keepdims=True)
+
+    def sum_all(number, *parts):
+        for place, part in enumerate(parts):
+            row = to_row(jnp.sum(part, axis=1, keepdims=True))
+            outbox[number, place : place + 1, 0:rhs] = row
+        if number == 0:
+            pl.semaphore_wait(barrier, total - 1)
+        copies = []
+        for slot, (index, device) in enumerate(others):
+            copy = pltpu.make_async_remote_copy(
+                src_ref=outbox.at[number],
+                dst_ref=inbox.at[number, here],
+                send_sem=send_sem.at[number, slot],
+                recv_sem=recv_sem.at[number, here],
+                device_id=device,
+                device_id_type=MESH,
+            )
+            copy.start()
+            copies.append(copy)
+        inbox[number, here] = outbox[number]
+        for slot, (index, device) in enumerate(others):
+            pltpu.make_async_remote_copy(
+                src_ref=outbox.at[number],
+                dst_ref=inbox.at[number, index],
+                send_sem=send_sem.at[number, slot],
+                recv_sem=recv_sem.at[number, index],
+                device_id=device,
+                device_id_type=MESH,
+            ).wait_recv()
+        for copy in copies:
+            copy.wait_send()
+        result = inbox[number, 0]
+        for index in range(1, total):
+            result = result + inbox[number, index]
+        return [to_column(result[place : place + 1, 0:rhs]) for place in range(len(parts))]
+
+    def sweep(terms, outputs):
+        sums = [jnp.zeros((rhs, width), jnp.float32)] * outputs
+        for block in range(blocks):
+            sums = [old + new for old, new in zip(sums, terms(block))]
+        return sums
+
+    start_square, start_image = sum_all(
+        0,
+        *sweep(
+            lambda k: (start_ref[k] * start_ref[k], start_ref[k] * image_ref[k]),
+            2,
+        ),
+    )
+    start_norm = jnp.sqrt(start_square + EPSILON)
+    scale = 1.0 / start_norm
+    along_first = start_image * scale * scale
+
+    def second_raw(k):
+        return (image_ref[k] - along_first * start_ref[k]) * scale
+
+    (rest_square,) = sum_all(1, *sweep(lambda k: (second_raw(k) * second_raw(k),), 1))
+    rest_first = jnp.sqrt(rest_square + EPSILON)
+    scale_two = 1.0 / rest_first
+    laplace_column = laplace_ref[...]
+
+    def cross(k):
+        first = start_ref[k] * scale
+        second = second_raw(k) * scale_two
+        near_second = (near_image_ref[k] - along_first * near_start_ref[k]) * scale * scale_two
+        image_two = resist_ref[k] * second + laplace_column * near_second
+        kept[k] = image_two
+        return first * image_two, second * image_two
+
+    along_cross, along_second = sum_all(2, *sweep(cross, 2))
+
+    def remain(k):
+        first = start_ref[k] * scale
+        second = second_raw(k) * scale_two
+        rest = kept[k] - along_cross * first - along_second * second
+        return (rest * rest,)
+
+    (last_square,) = sum_all(3, *sweep(remain, 1))
+    rest_second = jnp.sqrt(last_square + EPSILON)
+    radius_one = jnp.sqrt(along_first * along_first + rest_first * rest_first)
+    cosine_one = along_first / radius_one
+    sine_one = rest_first / radius_one
+    upper_right = cosine_one * along_cross + sine_one * along_second
+    lower_right = cosine_one * along_second - sine_one * along_cross
+    radius_two = jnp.sqrt(lower_right * lower_right + rest_second * rest_second)
+    amount_two = -(lower_right / radius_two) * start_norm * sine_one / radius_two
+    amount_one = (start_norm * cosine_one - upper_right * amount_two) / radius_one
+    amounts_ref[...] = jnp.zeros_like(amounts_ref)
+    amounts_ref[0:1, 0:rhs] = to_row(amount_one * scale)
+    amounts_ref[1:2, 0:rhs] = to_row(along_first)
+    amounts_ref[2:3, 0:rhs] = to_row(amount_two * scale * scale_two)
+
+
+def finish(start, image, near_start, near_image, resist_own, laplace, count, number):
     total = 2 * count
     return pl.pallas_call(
-        partial(sum_kernel, count),
-        out_shape=jax.ShapeDtypeStruct(part.shape, part.dtype),
-        in_specs=[pl.BlockSpec(memory_space=pltpu.VMEM)],
+        partial(finish_kernel, count),
+        out_shape=jax.ShapeDtypeStruct((8, 128), jnp.float32),
+        in_specs=[pl.BlockSpec(memory_space=pltpu.VMEM)] * 6,
         out_specs=pl.BlockSpec(memory_space=pltpu.VMEM),
         scratch_shapes=[
-            pltpu.VMEM((total - 1,) + part.shape, part.dtype),
-            pltpu.SemaphoreType.DMA((total - 1,)),
-            pltpu.SemaphoreType.DMA((total - 1,)),
+            pltpu.VMEM((4, 8, 128), jnp.float32),
+            pltpu.VMEM((4, total, 8, 128), jnp.float32),
+            pltpu.VMEM(start.shape, jnp.float32),
+            pltpu.SemaphoreType.DMA((4, total - 1)),
+            pltpu.SemaphoreType.DMA((4, total)),
         ],
         compiler_params=pltpu.CompilerParams(collective_id=number, has_side_effects=True),
-        name="sum_all",
-    )(part)
-
-
-def swap_kernel(mine_ref, both_ref, own_sem, send_sem, recv_sem):
-    brow, core = lax.axis_index("brow"), lax.axis_index("bcol")
-    other = (lax.axis_index("groups"), brow, 1 - core)
-    barrier = pltpu.get_barrier_semaphore()
-    pl.semaphore_signal(barrier, inc=1, device_id=other, device_id_type=MESH)
-    pl.semaphore_wait(barrier, 1)
-    copy = pltpu.make_async_remote_copy(
-        src_ref=mine_ref,
-        dst_ref=both_ref.at[core],
-        send_sem=send_sem,
-        recv_sem=recv_sem,
-        device_id=other,
-        device_id_type=MESH,
-    )
-    copy.start()
-    own = pltpu.make_async_copy(mine_ref, both_ref.at[core], own_sem)
-    own.start()
-    own.wait()
-    copy.wait()
-
-
-def swap_cores(mine, number):
-    return pl.pallas_call(
-        swap_kernel,
-        out_shape=jax.ShapeDtypeStruct((2,) + mine.shape, mine.dtype),
-        in_specs=[pl.BlockSpec(memory_space=pl.ANY)],
-        out_specs=pl.BlockSpec(memory_space=pl.ANY),
-        scratch_shapes=[pltpu.SemaphoreType.DMA] * 3,
-        compiler_params=pltpu.CompilerParams(collective_id=number, has_side_effects=True),
-        name="swap_cores",
-    )(mine)
+        name="finish",
+    )(start, image, near_start, near_image, resist_own, laplace)
 
 
 def multiply(vector, block_ref):
@@ -411,10 +461,8 @@
     return both[:rows] + (both[rows:] + rest)
 
 
-def build_kernel(first_row, count_ref, source_ref, target_ref, place_ref, order_ref, all_ref, near_ref, blocks_ref, buffer, sems):
-    width = near_ref.shape[2]
-    rows = near_ref.shape[1]
-    near_ref[...] = jnp.zeros_like(near_ref)
+def build_kernel(count_ref, source_ref, target_ref, order_ref, shape_ref, blocks_ref, buffer, sems):
+    width = shape_ref.shape[2]
     total = count_ref[0]
     tile = 64
 
@@ -429,8 +477,8 @@
             copy_out(slot, edge - 2).wait()
 
         source, target, order = source_ref[edge], target_ref[edge], order_ref[edge]
-        left = all_ref[source, rows : rows + 8, :]
-        right = all_ref[target, rows : rows + 8, :]
+        left = shape_ref[source]
+        right = shape_ref[target]
         tangent_left = jnp.transpose(left)
 
         for level in range(3):
@@ -486,8 +534,6 @@
                     buffer[slot, width + start : width + start + tile, :] = fine
 
         copy_out(slot, edge).start()
-        place = place_ref[edge]
-        near_ref[place] = near_ref[place] + multiply(all_ref[source, 0:rows, :], buffer.at[slot])
         return carry
 
     lax.fori_loop(0, total, one_edge, 0)
@@ -502,34 +548,87 @@
 
 
 DEPTH = 4
+BATCH = 4
 
 
 def apply_kernel(count_ref, source_ref, place_ref, all_ref, blocks_ref, near_ref, buffer, sems):
     near_ref[...] = jnp.zeros_like(near_ref)
     total = count_ref[0]
-
-    def copy_in(edge):
-        slot = lax.rem(edge, DEPTH)
-        return pltpu.make_async_copy(blocks_ref.at[edge], buffer.at[slot], sems.at[slot])
-
-    for edge in range(DEPTH - 1):
-
-        @pl.when(edge < total)
+    batches = (total + BATCH - 1) // BATCH
+
+    def copy_in(batch):
+        slot = lax.rem(batch, DEPTH)
+        return pltpu.make_async_copy(
+            blocks_ref.at[pl.ds(batch * BATCH, BATCH)], buffer.at[slot], sems.at[slot]
+        )
+
+    for batch in range(DEPTH - 1):
+
+        @pl.when(batch < batches)
         def _():
-            copy_in(jnp.int32(edge)).start()
-
-    def one_edge(edge, carry):
-        @pl.when(edge + DEPTH - 1 < total)
+            copy_in(jnp.int32(batch)).start()
+
+    def one_batch(batch, carry):
+        @pl.when(batch + DEPTH - 1 < batches)
         def _():
-            copy_in(edge + DEPTH - 1).start()
-
-        copy_in(edge).wait()
-        place = place_ref[edge]
-        slot = lax.rem(edge, DEPTH)
-        near_ref[place] = near_ref[place] + multiply(all_ref[source_ref[edge]], buffer.at[slot])
+            copy_in(batch + DEPTH - 1).start()
+
+        copy_in(batch).wait()
+        slot = lax.rem(batch, DEPTH)
+        terms = []
+        for step in range(BATCH):
+            edge = batch * BATCH + step
+            term = multiply(all_ref[source_ref[edge]], buffer.at[slot, step])
+            terms.append((place_ref[edge], jnp.where(edge < total, term, 0.0)))
+        for place, term in terms:
+            near_ref[place] = near_ref[place] + term
         return carry
 
-    lax.fori_loop(0, total, one_edge, 0)
+    lax.fori_loop(0, batches, one_batch, 0)
+
+
+SMEM_SPEC = pl.BlockSpec(memory_space=pltpu.SMEM)
+HBM_SPEC = pl.BlockSpec(memory_space=pl.ANY)
+
+
+def call_build(count, source, target, order, everything):
+    blocks, rows, width = everything.shape
+    room = source.shape[0]
+    return pl.pallas_call(
+        build_kernel,
+        grid=(1,),
+        out_shape=jax.ShapeDtypeStruct((room, 2 * width, width), jnp.bfloat16),
+        in_specs=[SMEM_SPEC] * 4
+        + [pl.BlockSpec((blocks, 8, width), lambda step: (0, rows // 8 - 1, 0))],
+        out_specs=HBM_SPEC,
+        scratch_shapes=[
+            pltpu.VMEM((2, 2 * width, width), jnp.bfloat16),
+            pltpu.SemaphoreType.DMA((2,)),
+        ],
+        compiler_params=pltpu.CompilerParams(vmem_limit_bytes=LIMIT),
+        name="build_blocks",
+    )(count, source, target, order, everything)
+
+
+def call_apply(count, source, place, everything, blocks, half, rhs_count):
+    width = everything.shape[2]
+    return pl.pallas_call(
+        apply_kernel,
+        grid=(1,),
+        out_shape=jax.ShapeDtypeStruct((half, rhs_count, width), jnp.float32),
+        in_specs=[SMEM_SPEC] * 3
+        + [
+            pl.BlockSpec((everything.shape[0], rhs_count, width), lambda step: (0, 0, 0)),
+            HBM_SPEC,
+        ],
+        out_specs=pl.BlockSpec(memory_space=pltpu.VMEM),
+        scratch_shapes=[
+            pltpu.VMEM((DEPTH, BATCH, 2 * width, width), jnp.bfloat16),
+            pltpu.SemaphoreType.DMA((DEPTH,)),
+        ],
+        compiler_params=pltpu.CompilerParams(vmem_limit_bytes=LIMIT),
+        name="apply_blocks",
+    )(count, source, place, everything, blocks)
 
 
 def edge_list(near_pairs, rule_orders, me, half, room):
@@ -570,13 +669,8 @@
     capacity = max(2, 2 * pair_count // owners)
     room = halves * pair_count + halves * owners * capacity
 
-    listed = lax.all_gather(
-        jnp.concatenate([near_pairs, rule_orders[:, None]], axis=1),
-        ("brow", "bcol"),
-        axis=0,
-        tiled=True,
-    )
-    count, source, target, place, order = edge_list(listed[:, 0:2], listed[:, 2], me, half, room)
+    room = -(-room // BATCH) * BATCH
+    here = lax.axis_index("brow")
 
     def own_half(array):
         rows = array.shape[0]
@@ -585,92 +679,43 @@
 
     start = own_half(right_sides)
     shape_own = own_half(geometry)
-    mine = jnp.concatenate([start, shape_own, jnp.zeros((half, 2, width), jnp.float32)], axis=1)
-    everything = gather_all(mine, owners, 0).reshape(all_blocks, rhs_count + 8, width)
-    smem = pl.BlockSpec(memory_space=pltpu.SMEM)
-    vmem = pl.BlockSpec(memory_space=pltpu.VMEM)
-    hbm = pl.BlockSpec(memory_space=pl.ANY)
-    near_shape = jax.ShapeDtypeStruct((half, rhs_count, width), jnp.float32)
-    near_start, blocks = pl.pallas_call(
-        partial(build_kernel, 0),
-        out_shape=(near_shape, jax.ShapeDtypeStruct((room, 2 * width, width), jnp.bfloat16)),
-        in_specs=[smem] * 5 + [vmem],
-        out_specs=(vmem, hbm),
-        scratch_shapes=[
-            pltpu.VMEM((2, 2 * width, width), jnp.bfloat16),
-            pltpu.SemaphoreType.DMA((2,)),
+    listed = jnp.concatenate([near_pairs[:, 0], near_pairs[:, 1], rule_orders])
+    listed = jnp.pad(listed.astype(jnp.float32), (0, width - 3 * pair_count))
+    spare = jnp.pad(listed.reshape(1, 1, width), ((0, half - 1), (0, 1), (0, 0)))
+    mine = jnp.concatenate([start, shape_own, spare], axis=1)
+    gathered = gather_all(mine, owners, 0)
+    everything = gathered.reshape(all_blocks, rhs_count + 8, width)
+    listed = gathered[:, 0, rhs_count + 6, :].astype(jnp.int32)
+    pairs = jnp.stack(
+        [
+            listed[:, 0:pair_count].reshape(-1),
+            listed[:, pair_count : 2 * pair_count].reshape(-1),
         ],
-        compiler_params=pltpu.CompilerParams(vmem_limit_bytes=LIMIT),
-        name="build_blocks",
-    )(count, source, target, place, order, everything)
-
+        axis=1,
+    )
+    orders = listed[:, 2 * pair_count : 3 * pair_count].reshape(-1)
+    count, source, target, place, order = edge_list(pairs, orders, me, half, room)
+    blocks = call_build(count, source, target, order, everything)
+    near_start = call_apply(count, source, place, everything, blocks, half, rhs_count)
     resist_own = lax.dynamic_slice_in_dim(resist, core * half * width, half * width, 0).reshape(
         half, 1, width
     )
-    laplace_rows = laplace.reshape(1, rhs_count, 1)
-
-    def spread(amount):
-        return amount[None, :, None]
-
-    def dots(number, *couples):
-        parts = [jnp.sum(left * right, axis=(0, 2)) for left, right in couples]
-        packed = jnp.zeros((8, 128), jnp.float32)
-        packed = packed.at[0 : len(parts), 0:rhs_count].set(jnp.stack(parts))
-        total = sum_all(packed, owners, number)
-        return [total[row, 0:rhs_count] for row in range(len(parts))]
-
-    image = resist_own * start + laplace_rows * near_start
+    image = resist_own * start + laplace.reshape(1, rhs_count, 1) * near_start
     everything_two = gather_all(image, owners, 1).reshape(all_blocks, rhs_count, width)
-    near_image = pl.pallas_call(
-        apply_kernel,
-        out_shape=near_shape,
-        in_specs=[smem] * 3 + [vmem, hbm],
-        out_specs=vmem,
-        scratch_shapes=[
-            pltpu.VMEM((DEPTH, 2 * width, width), jnp.bfloat16),
-            pltpu.SemaphoreType.DMA((DEPTH,)),
-        ],
-        compiler_params=pltpu.CompilerParams(vmem_limit_bytes=LIMIT),
-        name="apply_blocks",
-    )(count, source, place, everything_two, blocks)
-
-    start_square, start_image = dots(2, (start, start), (start, image))
-    start_norm = jnp.sqrt(start_square + EPSILON)
-    first = start / spread(start_norm)
-    along_first = start_image / start_norm / start_norm
-    second_raw = image / spread(start_norm) - spread(along_first) * first
-    (rest_square,) = dots(3, (second_raw, second_raw))
-    rest_first = jnp.sqrt(rest_square + EPSILON)
-    second = second_raw / spread(rest_first)
-    near_second = (
-        (near_image - spread(along_first) * near_start) / spread(start_norm) / spread(rest_first)
-    )
-    image_two = resist_own * second + laplace_rows * near_second
-    along_cross, along_second = dots(4, (first, image_two), (second, image_two))
-    remainder = image_two - spread(along_cross) * first - spread(along_second) * second
-    (last_square,) = dots(5, (remainder, remainder))
-    rest_second = jnp.sqrt(last_square + EPSILON)
-    radius_one = jnp.sqrt(along_first * along_first + rest_first * rest_first)
-    cosine_one = along_first / radius_one
-    sine_one = rest_first / radius_one
-    upper_right = cosine_one * along_cross + sine_one * along_second
-    lower_right = cosine_one * along_second - sine_one * along_cross
-    radius_two = jnp.sqrt(lower_right * lower_right + rest_second * rest_second)
-    amount_two = -(lower_right / radius_two) * start_norm * sine_one / radius_two
-    amount_one = (start_norm * cosine_one - upper_right * amount_two) / radius_one
-    combined = spread(amount_one) * first + spread(amount_two) * second
-    return (
-        swap_cores(combined, 6)
-        .reshape(blocks_here, rhs_count, width)
-        .transpose(1, 0, 2)
-        .reshape(rhs_count, blocks_here * width)
-    )
+    near_image = call_apply(count, source, place, everything_two, blocks, half, rhs_count)
+    amounts = finish(
+        start, image, near_start, near_image, resist_own, laplace.reshape(rhs_count, 1), owners, 2
+    )
+    own_image = lax.dynamic_slice_in_dim(everything_two, here * blocks_here, blocks_here, 0)
+    own_image = own_image.transpose(1, 0, 2).reshape(rhs_count, blocks_here * width)
+    amounts = amounts[0:3, 0:rhs_count, None]
+    return amounts[0] * right_sides + amounts[2] * (own_image - amounts[1] * right_sides)
 
 
 def body(near_pairs, rule_orders, geometry, resist, laplace, right_sides):
     owners = lax.axis_size("brow")
     blocks = geometry.shape[1] // BS * owners
-    if owners == 8 and lax.axis_size("bcol") == 2 and blocks <= 256:
+    if owners == 8 and lax.axis_size("bcol") == 2 and blocks <= 256 and near_pairs.shape[0] <= 85:
         return gather_body(near_pairs, rule_orders, geometry, resist, laplace, right_sides)
     return plain_body(near_pairs, rule_orders, geometry, resist, laplace, right_sides)
 

time: 380 us -> 298 us (0.78)
  the two profiles are of different devices: /device:TPU:0 before, /device:TPU:5 now
where the time goes in v2:
time: 298 us; the launch traced here: 295 us
  Pallas kernels  282 us (95%)
  other arithmetic  7.55 us (3%)
  local copies, waits for them, and re-layouts  5.29 us (2%)
    pallas_call x2, Pallas kernels, gather_all(): pl.pallas_call(partial(gather_kernel, count), out_shape=jax.ShapeDtypeStr...  138 us
    pallas_call x1, Pallas kernels, call_build(): pl.pallas_call(build_kernel, grid=(1,), out_shape=jax.ShapeDtypeStruct((r...  82.9 us
    pallas_call x2, Pallas kernels, call_apply(): pl.pallas_call(apply_kernel, grid=(1,), out_shape=jax.ShapeDtypeStruct((h...  34.3 us
    pallas_call x1, Pallas kernels, finish(): pl.pallas_call(partial(finish_kernel, count), out_shape=jax.ShapeDtypeStr...  27 us

profile of v2, /device:TPU:5, one launch (start us, length us, event | category | flops | bytes accessed | tf_op | source)
XLA Modules:
  0.0 295.4 jit_solution(2627005390672024493)
XLA Ops:
  0.0 0.0 copy-start
  0.0 1.1 constant_dynamic-slice_fusion.1
  1.2 0.0 copy-start.1
  1.2 0.0 copy-done
  1.2 0.8 slice_bitcast_fusion.4
  2.0 0.7 add_convert_fusion
  2.8 0.9 select_maximum_fusion.mine_ref
  3.7 56.1 %gather_all.2 = f32[16,16,40,256]{3,2,1,0:T(8,128)} custom-call(f32[16,40,256]{2,1,0:T(8,128)} %select_maximum_fusion.mine_ref), custom_call_target="tpu_custom_call" | custom-call | tf_op jit(solution)/shard_map/gather_all/pallas_call | solution.py:295
  59.7 0.9 slice_convert_fusion
  60.7 0.1 fusion.24
  60.7 0.1 squeeze_stack_reshape.6
  60.8 0.1 squeeze_stack_reshape.7
  60.9 0.1 convert_reduce_fusion
  61.0 0.2 convolution_bitcast_fusion
  61.2 0.1 fusion.2
  61.4 0.1 concatenate.43
  61.5 0.4 select_reduce_fusion
  61.9 0.6 broadcast_add_fusion
  62.5 0.6 convert_reduce_fusion.1
  63.2 82.9 %build_blocks.1.blocks_ref = bf16[384,512,256]{2,1,0:T(8,128)(2,1)} custom-call(s32[1]{0:T(128)} %bitcast.6.count_ref, s32[384]{0:T(512)} %get-tuple-element.16.source_ref, s32[384]{0:T(512)} %get-tuple-element.5.target_ref, s32[384]{0:T(512)} %get-tuple-element.15.order_ref, f32[256,40,256]{2,1,0:T(8,128)} %bitcast.50), custom_call_target="tpu_custom_call" | custom-call | tf_op jit(solution)/shard_map/build_blocks/pallas_call | solution.py:597
  146.0 0.0 copy-done.1
  146.0 0.0 copy-start.4
  146.0 0.0 copy-start.5
  146.1 17.1 %apply_blocks.2.near_start_ref = f32[16,32,256]{2,1,0:T(8,128)} custom-call(s32[1]{0:T(128)} %bitcast.6.count_ref, s32[384]{0:T(512)} %get-tuple-element.16.source_ref, s32[384]{0:T(512)} %get-tuple-element.6.place_ref, f32[256,40,256]{2,1,0:T(8,128)} %bitcast.51, bf16[384,512,256]{2,1,0:T(8,128)(2,1)} %build_blocks.1.blocks_ref), custom_call_target="tpu_custom_call" | custom-call | tf_op jit(solution)/shard_map/apply_blocks/pallas_call | solution.py:615
  163.2 0.0 copy-done.4
  163.2 0.0 copy-start.3
  163.3 0.0 copy-done.5
  163.3 2.0 multiply_add_fusion.1.mine_ref.image_ref
  165.3 81.8 %gather_all.3 = f32[16,16,32,256]{3,2,1,0:T(8,128)} custom-call(f32[16,32,256]{2,1,0:T(8,128)} %multiply_add_fusion.1.mine_ref.image_ref), custom_call_target="tpu_custom_call" | custom-call | tf_op jit(solution)/shard_map/gather_all/pallas_call | solution.py:295
  247.1 0.0 copy-start.2
  247.1 17.2 %apply_blocks.3.near_image_ref = f32[16,32,256]{2,1,0:T(8,128)} custom-call(s32[1]{0:T(128)} %bitcast.6.count_ref, s32[384]{0:T(512)} %get-tuple-element.16.source_ref, s32[384]{0:T(512)} %get-tuple-element.6.place_ref, f32[256,32,256]{2,1,0:T(8,128)} %bitcast.52, bf16[384,512,256]{2,1,0:T(8,128)(2,1)} %build_blocks.1.blocks_ref), custom_call_target="tpu_custom_call" | custom-call | tf_op jit(solution)/shard_map/apply_blocks/pallas_call | solution.py:615
  264.3 0.0 copy-done.3
  264.3 0.7 copy.12.laplace_ref
  265.0 27.0 %finish.1 = f32[8,128]{1,0:T(8,128)} custom-call(f32[16,32,256]{2,1,0:T(8,128)} %bitcast.55, f32[16,32,256]{2,1,0:T(8,128)} %multiply_add_fusion.1.mine_ref.image_ref, f32[16,32,256]{2,1,0:T(8,128)} %apply_blocks.2.near_start_ref, f32[16,32,256]{2,1,0:T(8,128)} %apply_blocks.3.near_image_ref, f32[16,1,256]{2,1,0:T(1,128)} %bitcast.60, f32[32,1]{1,0:T(8,128)} %copy.12.laplace_ref), custom_call_target="tpu_custom_call" | custom-call | tf_op jit(solution)/shard_map/finish/pallas_call | solution.py:433
  291.9 0.8 slice_bitcast_fusion.2
  292.7 1.3 dynamic-slice_bitcast_fusion
  294.1 0.1 copy.16
  294.2 0.0 copy-done.2
  294.2 1.2 multiply_add_fusion
  (11 shorter events, 0.1 us)
Async XLA Ops:
  0.0 1.2 copy-start
  1.2 144.8 %copy-start.1 = (f32[4,16,8,256]{3,2,0,1:T(8,128)}, f32[4,16,8,256]{3,2,0,1:T(8,128)S(1)}, u32[]{:S(2)}) copy-start(f32[4,16,8,256]{3,2,0,1:T(8,128)S(1)} %copy.21) | copy-start | bytes 1572868
  146.0 17.2 %copy-start.4 = (f32[8192]{0:T(1024)S(1)}, f32[8192]{0:T(1024)}, u32[]{:S(2)}) copy-start(f32[8192]{0:T(1024)} %param.9) | copy-start | bytes 98308
  146.0 17.2 %copy-start.5 = (f32[32]{0:T(128)S(1)}, f32[32]{0:T(128)}, u32[]{:S(2)}) copy-start(f32[32]{0:T(128)} %param.10) | copy-start | bytes 388
  163.2 101.0 %copy-start.3 = (f32[4096]{0:T(1024)}, f32[4096]{0:T(1024)S(1)}, u32[]{:S(2)}) copy-start(f32[4096]{0:T(1024)S(1)} %dynamic_slice.13) | copy-start | bytes 49156
  247.1 47.1 %copy-start.2 = (f32[32,8192]{1,0:T(8,128)S(1)}, f32[32,8192]{1,0:T(8,128)}, u32[]{:S(2)}) copy-start(f32[32,8192]{1,0:T(8,128)} %param.11) | copy-start | bytes 3145732
